TPU v7x, 32 devices: a whole 2x2x4 slice. The times are simulated.
32 devices in a mesh: groups: 2 (over x), dom: 16 (over z, y, core).
Axes of the slice: x: 2, y: 2, z: 4, core: 2. Of those that a mesh axis runs over, the one named last changes fastest.
Arguments:
- thickness: float32 [16, 8192], P(None, ('groups', 'dom')), parts along dimension 1, may hold values from 1 to 2
- tracers: float32 [3, 16, 8192], P(None, None, ('groups', 'dom')), parts along dimension 2, may hold values from 0 to 1
- velocity: float32 [2, 16, 8192], P(None, None, ('groups', 'dom')), parts along dimension 2, may hold values from -0.05 to 0.05
- max_level: int32 [7552], P('dom'), may hold values from 0 to 16, as said below
- cells_on_cell: int32 [6, 7552], P(None, 'dom'), may hold values from 0 to 472, as said below
- peer_ids: int32 [16, 8], P('dom'), may hold values from 0 to 15, as said below
- send_ids: int32 [16, 8, 48], P('dom'), may hold values from 0 to 255, as said below
- recv_pos: int32 [16, 8, 48], P('dom'), may hold values from 256 to 472, as said below
Outputs:
- new_thickness: float32 [16, 8192], P(None, ('groups', 'dom')), parts along dimension 1
- new_tracers: float32 [3, 16, 8192], P(None, None, ('groups', 'dom')), parts along dimension 2
There are 2 independent parts, one for each index of `groups`. A program takes and returns all parts, laid end to end along the dimension named above; an argument that names none is the same for every part. Nothing has to cross between parts.
Inputs may be any that keep to these rules, and one draw needn't show every extreme that they name: Layers below max_level are ocean; 0 marks land. Owned cells come first, then halo cells cycle by cycle; a halo cell carries the value of the cell it copies. `cells_on_cell`: entry j names the neighbour in the direction at j * 60 degrees, as a local id; 472 where the neighbour lies beyond the third cycle. Halo positions run from 256, cycle 1 first, then cycles 2 and 3. `peer_ids`: the peers of partition i are i + 1, i - 1, i + 3, i - 3, i + 4, i - 4, i + 5, i - 5, modulo 16, each once, in an order that varies by partition. `send_ids`: owned local ids that partition i sends to peer_ids[i, t], cycle 1 cells first, then cycle 2, then cycle 3; a cycle r cell stands within the first r * 16 slots; slots past the list hold 0. `recv_pos`: slot s of row t: where the s-th cell that peer_ids[i, t] sends to i lands; 472 past the list.
All inputs are finite; a program needn't handle non-finite values.
Results may differ from a plain program's by a relative error of at most 0.0003.
Values sent between devices are 32-bit elements; how exact they have to be, the bound alone decides.
A program may use at most 64 MiB of HBM per device.

v0:
```python
import functools
import math

import jax
import jax.numpy as jnp
from jax import lax
from jax.experimental import pallas as pl
from jax.experimental.pallas import tpu as pltpu
from jax.sharding import PartitionSpec as P

PGX = 4
OFFSETS = (PGX + 1, -PGX - 1, PGX, -PGX, PGX - 1, 1 - PGX, 1, -1)
THIRD_ORDER = 0.25
LIMIT_FLOOR = 1e-10
F32 = jnp.float32
BF16 = jnp.bfloat16
SPAN = 16
BLOCK = 8 * SPAN


def dot(a, b):
    return jnp.dot(a, b, preferred_element_type=F32)


def dot_nt(a, b):
    return lax.dot_general(a, b, (((1,), (1,)), ((), ())), preferred_element_type=F32)


def pieces(x):
    hi = x.astype(BF16)
    lo = (x - hi.astype(F32)).astype(BF16)
    return jnp.concatenate([hi, lo], axis=0)


def joined(x):
    half = x.shape[0] // 2
    return x[:half] + x[half:]


def one_hot(a, b):
    return jnp.where(a == b, 1.0, 0.0).astype(BF16)


def iota(shape, dim):
    return lax.broadcasted_iota(jnp.int32, shape, dim)


def peer_rows(peer, me, partitions, sign, table):
    o = iota((BLOCK, 8), 0) // SPAN
    offset = jnp.zeros((BLOCK, 8), jnp.int32)
    for at, value in enumerate(OFFSETS):
        offset = jnp.where(o == at, sign * value, offset)
    target = me + offset
    target = jnp.where(target >= partitions, target - partitions, target)
    target = jnp.where(target < 0, target + partitions, target)
    chosen = jnp.where(peer == target, 1.0, 0.0)
    return dot(chosen, table)


def slot_columns(rows, block, width):
    slots = rows.shape[1]
    row = iota((BLOCK, slots), 0) % SPAN
    lane = iota((BLOCK, slots), 1)
    own = jnp.where(lane == row + block * SPAN, rows, 0.0)
    return dot(own, jnp.ones((slots, width), F32))


def edges(h, q, vx, vy, curve, opened, far, far_curve, width):
    layers = h.shape[0]
    curves = [curve[m * layers : (m + 1) * layers] for m in range(3)]
    sum_flow = jnp.zeros_like(h)
    sum_low = [jnp.zeros_like(h) for _ in range(3)]
    inflow = [jnp.zeros_like(h) for _ in range(3)]
    outflow = [jnp.zeros_like(h) for _ in range(3)]
    upper = list(q)
    lower = list(q)
    antis = []
    for j in range(6):
        cols = slice(j * width, (j + 1) * width)
        heading = j * math.pi / 3.0
        part = lambda i: far[i * layers : (i + 1) * layers, cols]
        op = opened[:, cols]
        along = math.cos(heading) * (vx + part(4))
        across = math.sin(heading) * (vy + part(5))
        u = op * (along + across) * 0.5 * ((h + part(3)) * 0.5)
        sum_flow = sum_flow + u
        up = jnp.maximum(u, 0.0)
        un = jnp.minimum(u, 0.0)
        ua = THIRD_ORDER * jnp.abs(u)
        row = []
        for m in range(3):
            qn = part(m)
            ln = far_curve[m * layers : (m + 1) * layers, cols]
            low = up * q[m] + un * qn
            high = u * (0.5 * (q[m] + qn) - (curves[m] + ln) / 12.0) + ua * (ln - curves[m]) / 12.0
            sum_low[m] = sum_low[m] + low
            reached = jnp.where(op > 0, qn, q[m])
            upper[m] = jnp.maximum(upper[m], reached)
            lower[m] = jnp.minimum(lower[m], reached)
            a = high - low
            inflow[m] = inflow[m] + jnp.maximum(-a, 0.0)
            outflow[m] = outflow[m] + jnp.maximum(a, 0.0)
            row.append(a)
        antis.append(row)
    depth = h - sum_flow
    lowq, lim_in, lim_out = [], [], []
    for m in range(3):
        low = (h * q[m] - sum_low[m]) / depth
        lowq.append(low)
        lim_in.append(jnp.minimum(1.0, (upper[m] - low) * depth / (inflow[m] + LIMIT_FLOOR)))
        lim_out.append(jnp.minimum(1.0, (low - lower[m]) * depth / (outflow[m] + LIMIT_FLOOR)))
    return depth, lowq, lim_in, lim_out, antis


def curvature(q, far_q, opened, width):
    layers = opened.shape[0]
    out = []
    for m in range(3):
        rows = slice(m * layers, (m + 1) * layers)
        total = jnp.zeros((layers, width), F32)
        for j in range(6):
            cols = slice(j * width, (j + 1) * width)
            total = total + opened[:, cols] * (far_q[rows, cols] - q[m])
        out.append(total)
    return jnp.concatenate(out, axis=0)


def kernel(
    partitions,
    h_hbm,
    q_hbm,
    v_hbm,
    level_hbm,
    coc_hbm,
    peer_hbm,
    send_hbm,
    place_hbm,
    depth_ref,
    tracer_ref,
    h_ref,
    q_ref,
    v_ref,
    level_ref,
    coc_ref,
    peer_ref,
    send_ref,
    place_ref,
    load_sem,
    sent,
    came,
    table,
    g_own,
    g_b0,
    g_b1,
    far_own,
    far_b0,
    send_sem,
    recv_sem,
):
    loads = [
        pltpu.make_async_copy(src, dst, load_sem.at[at])
        for at, (src, dst) in enumerate(
            (
                (peer_hbm, peer_ref),
                (send_hbm, send_ref),
                (q_hbm, q_ref),
                (h_hbm, h_ref),
                (v_hbm, v_ref),
                (place_hbm, place_ref),
                (coc_hbm, coc_ref),
                (level_hbm, level_ref),
            )
        )
    ]
    for load in loads:
        load.start()
    layers, owned = h_ref.shape
    local = coc_ref.shape[1]
    halo = local - owned
    qrows = 3 * layers
    me = lax.axis_index("dom")
    targets = [lax.rem(me + (offset + partitions), partitions) for offset in OFFSETS]
    barrier = pltpu.get_barrier_semaphore()
    for target in targets:
        pl.semaphore_signal(
            barrier, inc=1, device_id={"dom": target}, device_id_type=pl.DeviceIdType.MESH
        )

    for load in loads[:5]:
        load.wait()

    peer = peer_ref[...]
    q = [q_ref[m] for m in range(3)]
    h = h_ref[...]
    vx = v_ref[0]
    vy = v_ref[1]
    fields = jnp.concatenate([q[0], q[1], q[2], h, vx, vy], axis=0)
    fields2 = pieces(fields)
    rows96 = 6 * layers
    blank = jnp.zeros((rows96, owned), BF16)
    edge = jnp.zeros((2 * layers, owned), BF16)
    edge1 = jnp.zeros((layers, owned), BF16)
    hi, lo = fields2[:rows96], fields2[rows96:]
    send_rows = peer_rows(peer, me, partitions, 1, send_ref[0].astype(F32))
    lane = iota((BLOCK, owned), 1).astype(F32)
    picks = [one_hot(slot_columns(send_rows, b, owned), lane) for b in range(3)]
    pay = []
    for b in range(2):
        total = None
        for piece in (hi, lo):
            main = jnp.concatenate([piece, edge], axis=0)
            if b == 0:
                tail = jnp.concatenate([blank, piece[: 2 * layers]], axis=0)
            else:
                tail = jnp.concatenate([blank, piece[2 * layers : qrows], edge1], axis=0)
            term = dot_nt(picks[b], main) + dot_nt(picks[2], tail)
            total = term if total is None else total + term
        pay.append(total)
    for p in range(8):
        sent[p, 0:SPAN] = pay[0][p * SPAN : (p + 1) * SPAN]
        sent[p, SPAN : 2 * SPAN] = pay[1][p * SPAN : (p + 1) * SPAN]
    pl.semaphore_wait(barrier, 8)
    copies = []
    for p in range(8):
        copy = pltpu.make_async_remote_copy(
            src_ref=sent.at[p],
            dst_ref=came.at[p],
            send_sem=send_sem.at[p],
            recv_sem=recv_sem.at[p],
            device_id={"dom": targets[p]},
            device_id_type=pl.DeviceIdType.MESH,
        )
        copy.start()
        copies.append(copy)

    for load in loads[5:]:
        load.wait()

    place_rows = peer_rows(peer, me, partitions, -1, (place_ref[0] - owned).astype(F32))
    keys = [slot_columns(place_rows, b, owned) for b in range(3)]
    keys = [jnp.where(key == float(halo), -4096.0, key) for key in keys]
    table[...] = jnp.zeros_like(table)
    table[0:6, 0:halo] = coc_ref[:, owned:local].astype(F32)
    table[8:9, 0:halo] = level_ref[:, owned:local].astype(F32)
    entries = table[...]
    above = jnp.where(entries >= float(owned), 1.0, 0.0)
    parts = jnp.concatenate([above, entries - above * float(owned)], axis=0).astype(BF16)
    width_t = table.shape[1]
    lane_t = iota((BLOCK, width_t), 1).astype(F32)
    found = []
    for b in range(3):
        got = dot_nt(parts, one_hot(keys[b][:, :width_t], lane_t))
        found.append(got[:16] * float(owned) + got[16:])
    own_idx = coc_ref[:, 0:owned].astype(F32)
    own_rows = iota((owned, owned), 0).astype(F32)
    for j in range(6):
        idx = own_idx[j : j + 1]
        cols = slice(j * owned, (j + 1) * owned)
        g_own[0:owned, cols] = one_hot(own_rows, idx)
        g_own[owned : owned + BLOCK, cols] = one_hot(keys[0], idx - float(owned))
        cols = slice(j * BLOCK, (j + 1) * BLOCK)
        idx = found[0][j : j + 1]
        g_b0[0:owned, cols] = one_hot(own_rows[:, :BLOCK], idx)
        for b in range(3):
            rows = slice(owned + b * BLOCK, owned + (b + 1) * BLOCK)
            g_b0[rows, cols] = one_hot(keys[b][:, :BLOCK], idx - float(owned))
        idx = found[1][j : j + 1]
        for b in range(3):
            rows = slice(b * BLOCK, (b + 1) * BLOCK)
            g_b1[rows, cols] = one_hot(keys[b][:, :BLOCK], idx - float(owned))

    lev_own = jnp.broadcast_to(level_ref[:, 0:owned].astype(F32), (layers, owned))
    lev_b = [jnp.broadcast_to(found[b][8:9], (layers, BLOCK)) for b in range(3)]
    lev_all = jnp.concatenate([lev_own] + lev_b, axis=1).astype(BF16)

    def opens(near, far, width):
        deep = jnp.concatenate([near] * 6, axis=1)
        layer = iota((layers, 6 * width), 0).astype(F32)
        return jnp.where(layer < jnp.minimum(deep, far), 1.0, 0.0)

    open_own = opens(lev_own, dot(lev_all[:, : owned + BLOCK], g_own[...]), owned)
    open_b0 = opens(lev_b[0], dot(lev_all, g_b0[...]), BLOCK)
    open_b1 = opens(lev_b[1], dot(lev_all[:, owned:], g_b1[...]), BLOCK)

    far_own[...] = joined(dot(fields2, g_own[0:owned, :]))
    far_b0[...] = joined(dot(fields2, g_b0[0:owned, :]))

    for copy in copies:
        copy.wait_recv()

    got0 = jnp.transpose(came[:, 0:SPAN, :].reshape(BLOCK, 8 * layers))
    got1 = jnp.transpose(came[:, SPAN : 2 * SPAN, :].reshape(BLOCK, 8 * layers))
    f0 = got0[:rows96]
    f1 = got1[:rows96]
    q2 = jnp.concatenate([got0[rows96:], got1[rows96 : rows96 + layers]], axis=0)
    fq = pieces(jnp.concatenate([f0[:qrows], f1[:qrows], q2], axis=1))
    fv = pieces(jnp.concatenate([f0[qrows:], f1[qrows:]], axis=1))
    far_o = far_own[...] + joined(dot(pieces(f0), g_own[owned : owned + BLOCK, :]))
    far_b0q = far_b0[0:qrows] + joined(dot(fq, g_b0[owned:, :]))
    far_b0v = far_b0[qrows:] + joined(dot(fv, g_b0[owned : owned + 2 * BLOCK, :]))
    far_b1q = joined(dot(fq, g_b1[...]))

    def tracers_of(f):
        return [f[m * layers : (m + 1) * layers] for m in range(3)]

    q_b0 = tracers_of(f0)
    l_own = curvature(q, far_o, open_own, owned)
    l_b0 = curvature(q_b0, far_b0q, open_b0, BLOCK)
    l_b1 = curvature(tracers_of(f1), far_b1q, open_b1, BLOCK)
    l_all = pieces(jnp.concatenate([l_own, l_b0, l_b1], axis=1))
    lfar_own = joined(dot(l_all[:, : owned + BLOCK], g_own[...]))
    lfar_b0 = joined(dot(l_all, g_b0[0 : owned + 2 * BLOCK, :]))

    far_b = jnp.concatenate([far_b0q, far_b0v], axis=0)
    h0, vx0, vy0 = (f0[i * layers : (i + 1) * layers] for i in range(3, 6))
    depth, lowq, lim_in, lim_out, antis = edges(
        h, q, vx, vy, l_own, open_own, far_o, lfar_own, owned
    )
    _, _, in0, out0, _ = edges(h0, q_b0, vx0, vy0, l_b0, open_b0, far_b, lfar_b0, BLOCK)
    lims = pieces(
        jnp.concatenate(
            [jnp.concatenate([a, b], axis=1) for a, b in zip(lim_in + lim_out, in0 + out0)], axis=0
        )
    )
    rfar = joined(dot(lims, g_own[...]))
    depth_ref[...] = depth
    for m in range(3):
        total = jnp.zeros_like(depth)
        for j in range(6):
            cols = slice(j * owned, (j + 1) * owned)
            a = antis[j][m]
            far_in = rfar[m * layers : (m + 1) * layers, cols]
            far_out = rfar[(3 + m) * layers : (4 + m) * layers, cols]
            factor = jnp.where(
                a > 0, jnp.minimum(lim_out[m], far_in), jnp.minimum(lim_in[m], far_out)
            )
            total = total + factor * a
        tracer_ref[m] = lowq[m] - total / depth
    for copy in copies:
        copy.wait_send()


def store_kernel(depth_ref, tracer_ref, depth_hbm, tracer_hbm, sem):
    first = pltpu.make_async_copy(tracer_ref, tracer_hbm, sem.at[0])
    second = pltpu.make_async_copy(depth_ref, depth_hbm, sem.at[1])
    first.start()
    second.start()
    first.wait()
    second.wait()


def shards(
    partitions, thickness, tracers, velocity, max_level, cells_on_cell, peer_ids, send_ids, recv_pos
):
    layers, owned = thickness.shape
    args = (
        thickness,
        tracers,
        velocity,
        max_level.reshape(1, -1),
        cells_on_cell,
        peer_ids,
        send_ids,
        recv_pos,
    )
    args = tuple(pltpu.with_memory_space_constraint(arg, pltpu.HBM) for arg in args)
    outs = (
        jax.ShapeDtypeStruct(thickness.shape, F32),
        jax.ShapeDtypeStruct(tracers.shape, F32),
    )
    vmem = pl.BlockSpec(memory_space=pltpu.VMEM)
    hbm = pl.BlockSpec(memory_space=pltpu.HBM)
    results = pl.pallas_call(
        functools.partial(kernel, partitions),
        out_shape=tuple(pltpu.VMEM(out.shape, out.dtype) for out in outs),
        in_specs=[hbm] * 8,
        out_specs=[vmem] * 2,
        scratch_shapes=[pltpu.VMEM(arg.shape, arg.dtype) for arg in args]
        + [
            pltpu.SemaphoreType.DMA((8,)),
            pltpu.VMEM((8, 2 * SPAN, 8 * layers), F32),
            pltpu.VMEM((8, 2 * SPAN, 8 * layers), F32),
            pltpu.VMEM((16, owned), F32),
            pltpu.VMEM((owned + BLOCK, 6 * owned), BF16),
            pltpu.VMEM((owned + 3 * BLOCK, 6 * BLOCK), BF16),
            pltpu.VMEM((3 * BLOCK, 6 * BLOCK), BF16),
            pltpu.VMEM((6 * layers, 6 * owned), F32),
            pltpu.VMEM((6 * layers, 6 * BLOCK), F32),
            pltpu.SemaphoreType.DMA((8,)),
            pltpu.SemaphoreType.DMA((8,)),
        ],
        compiler_params=pltpu.CompilerParams(
            collective_id=0, has_side_effects=True, vmem_limit_bytes=40 * 1024 * 1024
        ),
    )(*args)
    return tuple(
        pl.pallas_call(
            store_kernel,
            out_shape=outs,
            in_specs=[vmem] * 2,
            out_specs=[hbm] * 2,
            scratch_shapes=[pltpu.SemaphoreType.DMA((2,))],
        )(*results)
    )


def solution(mesh):
    return jax.shard_map(
        functools.partial(shards, mesh.shape["dom"]),
        mesh=mesh,
        in_specs=(
            P(None, ("groups", "dom")),
            P(None, None, ("groups", "dom")),
            P(None, None, ("groups", "dom")),
            P("dom"),
            P(None, "dom"),
            P("dom", None),
            P("dom", None, None),
            P("dom", None, None),
        ),
        out_specs=(P(None, ("groups", "dom")), P(None, None, ("groups", "dom"))),
        check_vma=False,
    )
```

profile of v0, /device:TPU:0, one launch (start us, length us, event | category | flops | bytes accessed | tf_op | source)
XLA Modules:
  0.0 14.4 jit_solution(824096196467413185)
XLA Ops:
  0.6 11.1 %shard_map.95 = (f32[16,256]{1,0:T(8,128)S(1)}, f32[3,16,256]{2,1,0:T(8,128)S(1)}) custom-call(f32[16,256]{1,0:T(8,128)} %h_hbm.1, f32[3,16,256]{2,1,0:T(8,128)} %q_hbm.1, f32[2,16,256]{2,1,0:T(8,128)} %v_hbm.1, s32[1,472]{1,0:T(1,128)} %bitcast.1, s32[6,472]{1,0:T(8,128)} %coc_hbm.1, s32[1,8]{1,0:T(1,128)} %peer_hbm.1, s32[1,8,48]{2,1,0:T(8,128)} %send_hbm.1, ...), custom_call_target="tpu_custom_call" | custom-call | tf_op jit(solution)/shard_map/pallas_call | solution.py:373
  11.7 0.0 copy-start
  11.7 0.6 %copy-done = f32[3,16,256]{2,1,0:T(8,128)} copy-done((f32[3,16,256]{2,1,0:T(8,128)}, f32[3,16,256]{2,1,0:T(8,128)S(1)}, u32[]{:S(2)}) %copy-start) | copy-done | bytes 49176
  12.3 0.0 copy-start.1
  12.3 0.6 %copy-done.1 = f32[16,256]{1,0:T(8,128)} copy-done((f32[16,256]{1,0:T(8,128)}, f32[16,256]{1,0:T(8,128)S(1)}, u32[]{:S(2)}) %copy-start.1) | copy-done | bytes 16408
  12.9 1.5 %shard_map.96 = (f32[16,256]{1,0:T(8,128)}, f32[3,16,256]{2,1,0:T(8,128)}) custom-call(f32[16,256]{1,0:T(8,128)} %copy-done.1, f32[3,16,256]{2,1,0:T(8,128)} %copy-done), custom_call_target="tpu_custom_call" | custom-call | tf_op jit(solution)/shard_map/pallas_call | solution.py:397
Async XLA Ops:
  11.7 0.6 %copy-start = (f32[3,16,256]{2,1,0:T(8,128)}, f32[3,16,256]{2,1,0:T(8,128)S(1)}, u32[]{:S(2)}) copy-start(f32[3,16,256]{2,1,0:T(8,128)S(1)} %get-tuple-element.5.tracer_ref) | copy-start | bytes 147460
  12.3 0.6 %copy-start.1 = (f32[16,256]{1,0:T(8,128)}, f32[16,256]{1,0:T(8,128)S(1)}, u32[]{:S(2)}) copy-start(f32[16,256]{1,0:T(8,128)S(1)} %get-tuple-element.4.depth_ref) | copy-start | bytes 49156
where the time goes:
time: 14.6 us; the launch traced here: 14.4 us
  Pallas kernels  12.5 us (86%)
  local copies, waits for them, and re-layouts  1.2 us (8%)
  between operations  0.65 us (4%)
    pallas_call x1, Pallas kernels, shards(): pl.pallas_call(functools.partial(kernel, partitions), out_shape=tuple((pl...  11.1 us
    pallas_call x1, Pallas kernels, shards(): pl.pallas_call(store_kernel, out_shape=outs, in_specs=[vmem] * 2, out_spe...  1.45 us
    unnamed x4, local copies, waits for them, and re-layouts  1.2 us

commit v1 on v0

--- a/solution.py
+++ b/solution.py
@@ -393,6 +393,7 @@
             collective_id=0, has_side_effects=True, vmem_limit_bytes=40 * 1024 * 1024
         ),
     )(*args)
+    results = [pltpu.with_memory_space_constraint(out, pltpu.VMEM) for out in results]
     return tuple(
         pl.pallas_call(
             store_kernel,
@@ -400,6 +401,7 @@
             in_specs=[vmem] * 2,
             out_specs=[hbm] * 2,
             scratch_shapes=[pltpu.SemaphoreType.DMA((2,))],
+            compiler_params=pltpu.CompilerParams(vmem_limit_bytes=2 * 1024 * 1024),
         )(*results)
     )
 

time: 14.6 us -> 12.5 us (0.86)
  local copies, waits for them, and re-layouts: 1.2 us -> 0 us
  Pallas kernels: 12.5 us -> 11.7 us
    unnamed x4 -> x0, local copies, waits for them, and re-layouts: 1.2 us -> none
    pallas_call x1, Pallas kernels: 1.45 us -> 0.64 us  [shards(): pl.pallas_call(store_kernel, out_shape=outs, in_specs=[vmem] * 2, out_spe...]
where the time goes in v1:
time: 12.5 us; the launch traced here: 12.3 us
  Pallas kernels  11.7 us (94%)
  between operations  0.64 us (5%)
    pallas_call x1, Pallas kernels, shards(): pl.pallas_call(functools.partial(kernel, partitions), out_shape=tuple((pl...  11.1 us
    pallas_call x1, Pallas kernels, shards(): pl.pallas_call(store_kernel, out_shape=outs, in_specs=[vmem] * 2, out_spe...  0.64 us

profile of v1, /device:TPU:0, one launch (start us, length us, event | category | flops | bytes accessed | tf_op | source)
XLA Modules:
  0.0 12.3 jit_solution(17996057344754479238)
XLA Ops:
  0.6 11.1 %shard_map.95 = (f32[16,256]{1,0:T(8,128)S(1)}, f32[3,16,256]{2,1,0:T(8,128)S(1)}) custom-call(f32[16,256]{1,0:T(8,128)} %h_hbm.1, f32[3,16,256]{2,1,0:T(8,128)} %q_hbm.1, f32[2,16,256]{2,1,0:T(8,128)} %v_hbm.1, s32[1,472]{1,0:T(1,128)} %bitcast.1, s32[6,472]{1,0:T(8,128)} %coc_hbm.1, s32[1,8]{1,0:T(1,128)} %peer_hbm.1, s32[1,8,48]{2,1,0:T(8,128)} %send_hbm.1, ...), custom_call_target="tpu_custom_call" | custom-call | tf_op jit(solution)/shard_map/pallas_call | solution.py:373
  11.7 0.6 %shard_map.96 = (f32[16,256]{1,0:T(8,128)}, f32[3,16,256]{2,1,0:T(8,128)}) custom-call(f32[16,256]{1,0:T(8,128)S(1)} %get-tuple-element.4.depth_ref, f32[3,16,256]{2,1,0:T(8,128)S(1)} %get-tuple-element.5.tracer_ref), custom_call_target="tpu_custom_call" | custom-call | tf_op jit(solution)/shard_map/pallas_call | solution.py:398

commit v2 on v1

--- a/solution.py
+++ b/solution.py
@@ -9,7 +9,7 @@
 from jax.sharding import PartitionSpec as P
 
 PGX = 4
-OFFSETS = (PGX + 1, -PGX - 1, PGX, -PGX, PGX - 1, 1 - PGX, 1, -1)
+OFFSETS = (1, -1, PGX - 1, 1 - PGX, PGX, -PGX, PGX + 1, -PGX - 1)
 THIRD_ORDER = 0.25
 LIMIT_FLOOR = 1e-10
 F32 = jnp.float32
@@ -157,6 +157,18 @@
     send_sem,
     recv_sem,
 ):
+    layers, owned = h_ref.shape
+    local = coc_ref.shape[1]
+    halo = local - owned
+    qrows = 3 * layers
+    me = lax.axis_index("dom")
+    targets = [lax.rem(me + (offset + partitions), partitions) for offset in OFFSETS]
+    barrier = pltpu.get_barrier_semaphore()
+    for target in targets:
+        pl.semaphore_signal(
+            barrier, inc=1, device_id={"dom": target}, device_id_type=pl.DeviceIdType.MESH
+        )
+
     loads = [
         pltpu.make_async_copy(src, dst, load_sem.at[at])
         for at, (src, dst) in enumerate(
@@ -174,18 +186,6 @@
     ]
     for load in loads:
         load.start()
-    layers, owned = h_ref.shape
-    local = coc_ref.shape[1]
-    halo = local - owned
-    qrows = 3 * layers
-    me = lax.axis_index("dom")
-    targets = [lax.rem(me + (offset + partitions), partitions) for offset in OFFSETS]
-    barrier = pltpu.get_barrier_semaphore()
-    for target in targets:
-        pl.semaphore_signal(
-            barrier, inc=1, device_id={"dom": target}, device_id_type=pl.DeviceIdType.MESH
-        )
-
     for load in loads[:5]:
         load.wait()
 
@@ -298,7 +298,7 @@
     far_o = far_own[...] + joined(dot(pieces(f0), g_own[owned : owned + BLOCK, :]))
     far_b0q = far_b0[0:qrows] + joined(dot(fq, g_b0[owned:, :]))
     far_b0v = far_b0[qrows:] + joined(dot(fv, g_b0[owned : owned + 2 * BLOCK, :]))
-    far_b1q = joined(dot(fq, g_b1[...]))
+    far_b1q = dot(fq[:qrows], g_b1[...])
 
     def tracers_of(f):
         return [f[m * layers : (m + 1) * layers] for m in range(3)]
@@ -307,9 +307,9 @@
     l_own = curvature(q, far_o, open_own, owned)
     l_b0 = curvature(q_b0, far_b0q, open_b0, BLOCK)
     l_b1 = curvature(tracers_of(f1), far_b1q, open_b1, BLOCK)
-    l_all = pieces(jnp.concatenate([l_own, l_b0, l_b1], axis=1))
-    lfar_own = joined(dot(l_all[:, : owned + BLOCK], g_own[...]))
-    lfar_b0 = joined(dot(l_all, g_b0[0 : owned + 2 * BLOCK, :]))
+    l_all = jnp.concatenate([l_own, l_b0, l_b1], axis=1).astype(BF16)
+    lfar_own = dot(l_all[:, : owned + BLOCK], g_own[...])
+    lfar_b0 = dot(l_all, g_b0[0 : owned + 2 * BLOCK, :])
 
     far_b = jnp.concatenate([far_b0q, far_b0v], axis=0)
     h0, vx0, vy0 = (f0[i * layers : (i + 1) * layers] for i in range(3, 6))
@@ -317,12 +317,10 @@
         h, q, vx, vy, l_own, open_own, far_o, lfar_own, owned
     )
     _, _, in0, out0, _ = edges(h0, q_b0, vx0, vy0, l_b0, open_b0, far_b, lfar_b0, BLOCK)
-    lims = pieces(
-        jnp.concatenate(
-            [jnp.concatenate([a, b], axis=1) for a, b in zip(lim_in + lim_out, in0 + out0)], axis=0
-        )
-    )
-    rfar = joined(dot(lims, g_own[...]))
+    lims = jnp.concatenate(
+        [jnp.concatenate([a, b], axis=1) for a, b in zip(lim_in + lim_out, in0 + out0)], axis=0
+    )
+    rfar = dot(lims.astype(BF16), g_own[...])
     depth_ref[...] = depth
     for m in range(3):
         total = jnp.zeros_like(depth)

time: 12.5 us -> 12 us (0.960)
  Pallas kernels: 11.7 us -> 11.2 us
    pallas_call x1, Pallas kernels: 11.1 us -> 10.6 us  [shards(): pl.pallas_call(functools.partial(kernel, partitions), out_shape=tuple((pl...]
where the time goes in v2:
time: 12 us; the launch traced here: 11.9 us
  Pallas kernels  11.2 us (93%)
  between operations  0.64 us (5%)
    pallas_call x1, Pallas kernels, shards(): pl.pallas_call(functools.partial(kernel, partitions), out_shape=tuple((pl...  10.6 us
    pallas_call x1, Pallas kernels, shards(): pl.pallas_call(store_kernel, out_shape=outs, in_specs=[vmem] * 2, out_spe...  0.64 us

profile of v2, /device:TPU:0, one launch (start us, length us, event | category | flops | bytes accessed | tf_op | source)
XLA Modules:
  0.0 11.9 jit_solution(5112811585613800928)
XLA Ops:
  0.6 10.6 %shard_map.95 = (f32[16,256]{1,0:T(8,128)S(1)}, f32[3,16,256]{2,1,0:T(8,128)S(1)}) custom-call(f32[16,256]{1,0:T(8,128)} %h_hbm.1, f32[3,16,256]{2,1,0:T(8,128)} %q_hbm.1, f32[2,16,256]{2,1,0:T(8,128)} %v_hbm.1, s32[1,472]{1,0:T(1,128)} %bitcast.1, s32[6,472]{1,0:T(8,128)} %coc_hbm.1, s32[1,8]{1,0:T(1,128)} %peer_hbm.1, s32[1,8,48]{2,1,0:T(8,128)} %send_hbm.1, ...), custom_call_target="tpu_custom_call" | custom-call | tf_op jit(solution)/shard_map/pallas_call | solution.py:371
  11.2 0.6 %shard_map.96 = (f32[16,256]{1,0:T(8,128)}, f32[3,16,256]{2,1,0:T(8,128)}) custom-call(f32[16,256]{1,0:T(8,128)S(1)} %get-tuple-element.4.depth_ref, f32[3,16,256]{2,1,0:T(8,128)S(1)} %get-tuple-element.5.tracer_ref), custom_call_target="tpu_custom_call" | custom-call | tf_op jit(solution)/shard_map/pallas_call | solution.py:396

commit v3 on v2

--- a/solution.py
+++ b/solution.py
@@ -92,7 +92,7 @@
             qn = part(m)
             ln = far_curve[m * layers : (m + 1) * layers, cols]
             low = up * q[m] + un * qn
-            high = u * (0.5 * (q[m] + qn) - (curves[m] + ln) / 12.0) + ua * (ln - curves[m]) / 12.0
+            high = u * (0.5 * (q[m] + qn) - (curves[m] + ln)) + ua * (ln - curves[m])
             sum_low[m] = sum_low[m] + low
             reached = jnp.where(op > 0, qn, q[m])
             upper[m] = jnp.maximum(upper[m], reached)
@@ -103,13 +103,14 @@
             row.append(a)
         antis.append(row)
     depth = h - sum_flow
+    inverse = 1.0 / depth
     lowq, lim_in, lim_out = [], [], []
     for m in range(3):
-        low = (h * q[m] - sum_low[m]) / depth
+        low = (h * q[m] - sum_low[m]) * inverse
         lowq.append(low)
         lim_in.append(jnp.minimum(1.0, (upper[m] - low) * depth / (inflow[m] + LIMIT_FLOOR)))
         lim_out.append(jnp.minimum(1.0, (low - lower[m]) * depth / (outflow[m] + LIMIT_FLOOR)))
-    return depth, lowq, lim_in, lim_out, antis
+    return depth, inverse, lowq, lim_in, lim_out, antis
 
 
 def curvature(q, far_q, opened, width):
@@ -121,7 +122,7 @@
         for j in range(6):
             cols = slice(j * width, (j + 1) * width)
             total = total + opened[:, cols] * (far_q[rows, cols] - q[m])
-        out.append(total)
+        out.append(total * (1.0 / 12.0))
     return jnp.concatenate(out, axis=0)
 
 
@@ -313,10 +314,10 @@
 
     far_b = jnp.concatenate([far_b0q, far_b0v], axis=0)
     h0, vx0, vy0 = (f0[i * layers : (i + 1) * layers] for i in range(3, 6))
-    depth, lowq, lim_in, lim_out, antis = edges(
+    depth, inverse, lowq, lim_in, lim_out, antis = edges(
         h, q, vx, vy, l_own, open_own, far_o, lfar_own, owned
     )
-    _, _, in0, out0, _ = edges(h0, q_b0, vx0, vy0, l_b0, open_b0, far_b, lfar_b0, BLOCK)
+    _, _, _, in0, out0, _ = edges(h0, q_b0, vx0, vy0, l_b0, open_b0, far_b, lfar_b0, BLOCK)
     lims = jnp.concatenate(
         [jnp.concatenate([a, b], axis=1) for a, b in zip(lim_in + lim_out, in0 + out0)], axis=0
     )
@@ -333,7 +334,7 @@
                 a > 0, jnp.minimum(lim_out[m], far_in), jnp.minimum(lim_in[m], far_out)
             )
             total = total + factor * a
-        tracer_ref[m] = lowq[m] - total / depth
+        tracer_ref[m] = lowq[m] - total * inverse
     for copy in copies:
         copy.wait_send()
 

time: 12 us -> 12 us (level)
  no operation moved by 1% of the time
where the time goes in v3:
time: 12 us; the launch traced here: 11.9 us
  Pallas kernels  11.2 us (93%)
  between operations  0.64 us (5%)
    pallas_call x1, Pallas kernels, shards(): pl.pallas_call(functools.partial(kernel, partitions), out_shape=tuple((pl...  10.6 us
    pallas_call x1, Pallas kernels, shards(): pl.pallas_call(store_kernel, out_shape=outs, in_specs=[vmem] * 2, out_spe...  0.64 us

profile of v3, /device:TPU:0, one launch (start us, length us, event | category | flops | bytes accessed | tf_op | source)
XLA Modules:
  0.0 11.9 jit_solution(12718134229023854925)
XLA Ops:
  0.6 10.6 %shard_map.95 = (f32[16,256]{1,0:T(8,128)S(1)}, f32[3,16,256]{2,1,0:T(8,128)S(1)}) custom-call(f32[16,256]{1,0:T(8,128)} %h_hbm.1, f32[3,16,256]{2,1,0:T(8,128)} %q_hbm.1, f32[2,16,256]{2,1,0:T(8,128)} %v_hbm.1, s32[1,472]{1,0:T(1,128)} %bitcast.1, s32[6,472]{1,0:T(8,128)} %coc_hbm.1, s32[1,8]{1,0:T(1,128)} %peer_hbm.1, s32[1,8,48]{2,1,0:T(8,128)} %send_hbm.1, ...), custom_call_target="tpu_custom_call" | custom-call | tf_op jit(solution)/shard_map/pallas_call | solution.py:372
  11.2 0.6 %shard_map.96 = (f32[16,256]{1,0:T(8,128)}, f32[3,16,256]{2,1,0:T(8,128)}) custom-call(f32[16,256]{1,0:T(8,128)S(1)} %get-tuple-element.4.depth_ref, f32[3,16,256]{2,1,0:T(8,128)S(1)} %get-tuple-element.5.tracer_ref), custom_call_target="tpu_custom_call" | custom-call | tf_op jit(solution)/shard_map/pallas_call | solution.py:397
